TPU v7x, 256 devices: a whole 4x4x8 slice. The times are simulated.
256 devices in a mesh: front: 64 (over x, y, z_lo, core), blk: 4 (over z_hi).
Axes of the slice: x: 4, y: 4, z: 8 (z_hi: 4, z_lo: 2; z = z_hi * 2 + z_lo), core: 2. Of those that a mesh axis runs over, the one named last changes fastest.
Arguments:
- child_diag: float32 [65536, 1024], P(('front', 'blk')), as said below
- child_top: float32 [32768, 1024], P(('front', 'blk')), may hold values from -0.078125 to 0.078125
- child_rows: float32 [131072, 1024], P(('front', 'blk')), may hold values from -12 to 12
- row_owner: int32 [64, 16, 1], P('front'), may hold values from 0 to 63; in each aligned block of 16 rows (0 to 15, 16 to 31, ..., all dimensions but the last counted through in order) at most 2 rows name the same one
- row_slot: int32 [64, 16], P('front'), may hold values from 0 to 3
- col_block: int32 [64, 4], P('front'), may hold values from 0 to 1
- parent_diag: float32 [1024, 1024], P('blk'), as said below
- parent_rows: float32 [32768, 1024], P('front', 'blk'), may hold values from -6 to 6
Outputs:
- parent_factor: float32 [1024, 1024], P('blk')
- parent_panel: float32 [32768, 1024], P(('front', 'blk'))
Inputs may be any that keep to these rules, and one draw needn't show every extreme that they name: `row_owner`: within the 16 row blocks of one child no owner is named more than 2 times, and in some children one owner is named exactly 2 times. `child_diag`: each 1024 x 1024 block is symmetric with all eigenvalues at least 1. `parent_diag`: symmetric with all eigenvalues at least 24; parent_diag - diag_update has all eigenvalues at least 12.
All inputs are finite; a program needn't handle non-finite values.
Results may differ from a plain program's by a relative error of at most 0.0001.
Values sent between devices are 32-bit elements; how exact they have to be, the bound alone decides.
A program may use at most 192 MiB of HBM per device.

v0:
```python
import jax
import jax.numpy as jnp
from jax import lax
from jax.sharding import PartitionSpec as P

W = 1024
TILE = 128
TA = 4
PB = 4
HIGHEST = lax.Precision.HIGHEST


def right_solve(factor, matrix):
    return jax.scipy.linalg.solve_triangular(factor, matrix.T, lower=True).T


def blocked_cholesky(matrix):
    order_size = matrix.shape[0]
    stride = min(256, order_size)
    remaining = matrix
    factor = jnp.zeros_like(matrix)
    for offset in range(0, order_size, stride):
        finish = offset + stride
        diag_piece = jnp.linalg.cholesky(remaining[offset:finish, offset:finish])
        factor = factor.at[offset:finish, offset:finish].set(diag_piece)
        if finish < order_size:
            lower_part = right_solve(diag_piece, remaining[finish:, offset:finish])
            factor = factor.at[finish:, offset:finish].set(lower_part)
            trailing = remaining[finish:, finish:] - jnp.dot(
                lower_part, lower_part.T, precision=HIGHEST
            )
            remaining = remaining.at[finish:, finish:].set(trailing)
    return factor


def shards(
    child_diag, child_top, child_rows, row_owner, row_slot, col_block, parent_diag, parent_rows
):
    block_count = lax.axis_size("blk")
    front_count = lax.axis_size("front")
    my_block = lax.axis_index("blk")
    quarter = W // (TILE * block_count)
    block_width = W // TILE
    capacity = max(2, 8 * TA // front_count)
    diag_whole, top_whole = (
        lax.all_gather(child_diag, "blk", axis=0, tiled=True),
        lax.all_gather(child_top, "blk", axis=0, tiled=True),
    )
    factor = blocked_cholesky(diag_whole)
    top_solved = right_solve(factor, top_whole)
    rows_solved = right_solve(factor, child_rows)
    top_tiles = top_solved.reshape(block_count, TILE, W)
    schur_tiles = jnp.einsum("rw,kcw->krc", rows_solved, top_tiles, precision=HIGHEST)
    arrived = lax.all_to_all(schur_tiles, "blk", split_axis=0, concat_axis=0, tiled=True)
    arrived = arrived.reshape(block_count * TA, TILE, TILE)
    owners = row_owner[0, :, 0]
    slot_index = row_slot[0]
    column_picks = col_block[0]
    sequence = jnp.arange(owners.shape[0], dtype=jnp.int32)
    earlier = (owners[:, None] == owners[None, :]) & (sequence[None, :] < sequence[:, None])
    arrival_rank = jnp.sum(earlier.astype(jnp.int32), axis=1)
    position = owners * capacity + arrival_rank
    block_ids = jnp.arange(block_count, dtype=jnp.int32)
    my_pick = jnp.sum(jnp.where(block_ids == my_block, column_picks, 0))
    landing = slot_index * quarter + my_pick
    outgoing = (
        jnp.zeros((front_count * capacity, TILE, TILE), jnp.float32).at[position].set(arrived)
    )
    labels = jnp.zeros((front_count * capacity,), jnp.int32).at[position].set(landing)
    received, received_labels = (
        lax.all_to_all(
            outgoing.reshape(front_count, capacity, TILE, TILE),
            "front",
            split_axis=0,
            concat_axis=0,
            tiled=True,
        ),
        lax.all_to_all(
            labels.reshape(front_count, capacity), "front", split_axis=0, concat_axis=0, tiled=True
        ),
    )
    tile_sums = (
        jnp.zeros((PB * quarter, TILE, TILE), jnp.float32)
        .at[received_labels.reshape(-1)]
        .add(received.reshape(-1, TILE, TILE))
    )
    panel_update = (
        tile_sums.reshape(PB, quarter, TILE, TILE)
        .transpose(0, 2, 1, 3)
        .reshape(PB * TILE, quarter * TILE)
    )
    updated = parent_rows - panel_update
    row_major = lax.all_to_all(updated, "blk", split_axis=0, concat_axis=1, tiled=True)
    columns = block_ids * quarter + column_picks
    my_top = lax.dynamic_slice_in_dim(top_solved, my_block * TILE, TILE, 0)
    cross_terms = jnp.dot(my_top, top_solved.T, precision=HIGHEST)
    cross_terms = cross_terms.reshape(TILE, block_count, TILE).transpose(1, 0, 2)
    row_block = my_block * quarter + my_pick
    spread = (
        jnp.zeros((block_width, TILE, block_width, TILE), jnp.float32)
        .at[row_block, :, columns, :]
        .set(cross_terms)
    )
    owner_mask = jnp.where(lax.axis_index("front") == 0, 1.0, 0.0).astype(jnp.float32)
    placed = lax.dynamic_update_slice_in_dim(
        jnp.zeros((W, W), jnp.float32), parent_diag * owner_mask, my_block * quarter * TILE, 0
    )
    whole_diag = lax.psum(placed - spread.reshape(W, W), ("front", "blk"))
    parent_factor = blocked_cholesky(whole_diag)
    own_rows = lax.dynamic_slice_in_dim(parent_factor, my_block * quarter * TILE, quarter * TILE, 0)
    return (own_rows, right_solve(parent_factor, row_major))


def solution(mesh):
    return jax.shard_map(
        shards,
        mesh=mesh,
        in_specs=(
            P(("front", "blk"), None),
            P(("front", "blk"), None),
            P(("front", "blk"), None),
            P("front", None, None),
            P("front", None),
            P("front", None),
            P("blk", None),
            P("front", "blk"),
        ),
        out_specs=(P("blk", None), P(("front", "blk"), None)),
        check_vma=False,
    )
```

profile of v0, /device:TPU:2, one launch (start us, length us, event | category | flops | bytes accessed | tf_op | source)
XLA Modules:
  0.0 1292.2 jit_solution(12158726002848538924)
XLA Ops:
  12.9 81.6 %all-gather.3.cloned.1.call-done = f32[1024,1024]{0,1:T(8,128)} async-done(((f32[256,1024]{0,1:T(8,128)}), f32[1024,1024]{0,1:T(8,128)}) %all-gather.3.cloned.1.call-update) | async-done | bytes 4194320 | tf_op jit(solution)/shard_map/all_gather | solution.py:46
  96.6 11.7 cholesky.382
  108.4 9.8 custom-call.38
  118.7 11.7 cholesky.399
  136.4 20.1 %custom-call.39 = f32[2,128,128]{1,2,0:T(8,128)S(1)} custom-call(f32[2,128,128]{2,1,0:T(8,128)S(1)} %get-tuple-element.311), custom_call_target="InvertDiagBlocksLowerTriangular" | custom-call | tf_op jit(solution)/shard_map/jit(_solve_triangular)/triangular_solve | solution.py:14
  169.0 11.7 cholesky.416
  180.8 10.4 custom-call.40
  192.5 11.9 cholesky.433
  212.0 19.7 %custom-call.41 = f32[2,128,128]{1,2,0:T(8,128)S(1)} custom-call(f32[2,128,128]{2,1,0:T(8,128)S(1)} %get-tuple-element.312), custom_call_target="InvertDiagBlocksLowerTriangular" | custom-call | tf_op jit(solution)/shard_map/jit(_solve_triangular)/triangular_solve | solution.py:14
  238.9 11.7 cholesky.450
  250.6 9.8 custom-call.42
  260.9 11.7 cholesky.467
  280.3 20.1 %custom-call.43 = f32[2,128,128]{1,2,0:T(8,128)S(1)} custom-call(f32[2,128,128]{2,1,0:T(8,128)S(1)} %get-tuple-element.313), custom_call_target="InvertDiagBlocksLowerTriangular" | custom-call | tf_op jit(solution)/shard_map/jit(_solve_triangular)/triangular_solve | solution.py:14
  302.0 11.7 cholesky.484
  313.8 9.8 custom-call.44
  324.1 11.7 cholesky.501
  340.1 4.8 fusion.1
  344.9 23.0 %while.41 = (s32[]{:T(128)}, f32[1024,1024]{1,0:T(8,128)}, s32[8,2]{0,1:T(2,128)S(1)}, f32[8,128,128]{2,1,0:T(8,128)S(1)}, s32[]{:T(128)}) while((s32[]{:T(128)}, f32[1024,1024]{1,0:T(8,128)}, s32[8,2]{0,1:T(2,128)S(1)}, f32[8,128,128]{2,1,0:T(8,128)S(1)}, s32[]{:T(128)}) %tuple.338), condition=%wide.while_cond.23, body=%wide.while_body.23.sunk | while | flops 2 | bytes 131181 | solution.py:14
  367.9 78.8 %custom-call.45 = f32[8,128,128]{1,2,0:T(8,128)S(1)} custom-call(f32[8,128,128]{2,1,0:T(8,128)S(1)} %get-tuple-element.314), custom_call_target="InvertDiagBlocksLowerTriangular" | custom-call | tf_op jit(solution)/shard_map/jit(_solve_triangular)/triangular_solve | solution.py:14
  487.1 6.7 fusion.4
  493.8 9.4 all-to-all-start.1
  512.9 16.0 %all-to-all-done.1 = f32[4,512,128]{1,2,0:T(8,128)S(1)} async-done(((f32[4,512,128]{1,2,0:T(8,128)}), f32[4,512,128]{1,2,0:T(8,128)S(1)}, u32[]{:S(2)}, u32[]{:S(2)}) %all-to-all-start.1) | async-done | bytes 1048608 | tf_op jit(solution)/shard_map/all_to_all | solution.py:54
  528.9 10.3 all-to-all-start
  540.6 4.3 broadcast_in_dim.27
  547.8 9.0 all-to-all-start.2
  563.1 5.5 copy.213
  568.6 7.0 bitcast_subtract_fusion
  577.0 314.4 %all-reduce.6.cloned.1.call-done = f32[1024,1024]{0,1:T(8,128)} async-done(((f32[1024,1024]{0,1:T(8,128)}), f32[1024,1024]{0,1:T(8,128)}) %all-reduce.6.cloned.1.call-update) | async-done | bytes 4194320 | tf_op jit(solution)/shard_map/psum | solution.py:108
  893.4 11.7 cholesky.518
  905.3 9.8 custom-call.46
  915.7 11.7 cholesky.535
  935.4 19.7 %custom-call.47 = f32[2,128,128]{1,2,0:T(8,128)S(1)} custom-call(f32[2,128,128]{2,1,0:T(8,128)S(1)} %get-tuple-element.315), custom_call_target="InvertDiagBlocksLowerTriangular" | custom-call | tf_op jit(solution)/shard_map/jit(_solve_triangular)/triangular_solve | solution.py:14
  962.9 11.7 cholesky.552
  974.7 9.8 custom-call.48
  986.8 11.9 cholesky.569
  1010.9 19.7 %custom-call.49 = f32[2,128,128]{1,2,0:T(8,128)S(1)} custom-call(f32[2,128,128]{2,1,0:T(8,128)S(1)} %get-tuple-element.316), custom_call_target="InvertDiagBlocksLowerTriangular" | custom-call | tf_op jit(solution)/shard_map/jit(_solve_triangular)/triangular_solve | solution.py:14
  1033.3 11.7 cholesky.586
  1045.1 9.8 custom-call.50
  1055.5 12.1 cholesky.603
  1076.4 19.7 %custom-call.51 = f32[2,128,128]{1,2,0:T(8,128)S(1)} custom-call(f32[2,128,128]{2,1,0:T(8,128)S(1)} %get-tuple-element.317), custom_call_target="InvertDiagBlocksLowerTriangular" | custom-call | tf_op jit(solution)/shard_map/jit(_solve_triangular)/triangular_solve | solution.py:14
  1097.8 11.7 cholesky.620
  1109.6 9.8 custom-call.52
  1120.0 11.7 cholesky.637
  1136.0 4.7 fusion
  1140.8 17.2 %scatter_fusion.2 = f32[8,128,128]{2,1,0:T(8,128)S(1)} fusion(f32[8,128,128]{2,1,0:T(8,128)S(1)} %broadcast.606.clone.1, s32[128]{0:T(128)S(1)} %fusion.185, f32[128,128,128]{2,1,0:T(8,128)} %bitcast.84), kind=kCustom, calls=%fused_computation.3 | custom fusion | flops 2097152 | bytes 25166336 | tf_op jit(solution)/shard_map/scatter-add | solution.py:85
  1159.3 5.6 all-to-all-start.3
  1164.9 25.1 %while.37 = (s32[]{:T(128)}, f32[1024,1024]{0,1:T(8,128)}, s32[8,2]{0,1:T(2,128)S(1)}, f32[8,128,128]{2,1,0:T(8,128)S(1)}, s32[]{:T(128)}) while((s32[]{:T(128)}, f32[1024,1024]{0,1:T(8,128)}, s32[8,2]{0,1:T(2,128)S(1)}, f32[8,128,128]{2,1,0:T(8,128)S(1)}, s32[]{:T(128)}) %tuple.359), condition=%wide.while_cond.24, body=%wide.while_body.24.sunk | while | flops 2 | bytes 393321 | solution.py:14
  1189.9 78.6 %custom-call.24 = f32[8,128,128]{1,2,0:T(8,128)S(1)} custom-call(f32[8,128,128]{2,1,0:T(8,128)S(1)} %get-tuple-element.286), custom_call_target="InvertDiagBlocksLowerTriangular" | custom-call | tf_op jit(solution)/shard_map/jit(_solve_triangular)/triangular_solve | solution.py:14
  (402 shorter events, 249.5 us)
Async XLA Ops:
  7.2 2.8 copy-start.13
  7.2 3.9 copy-start.9
  7.2 87.3 %all-gather.3.cloned.1.call-start = ((), (), s32[]{:S(2)}) async-start(), calls=%async_computation.4 | async-start | bytes 5242880 | tf_op jit(solution)/shard_map/all_gather | solution.py:46
  9.9 456.9 %all-gather.5.cloned.1.call-start = ((), (), s32[]{:S(2)}) async-start(), calls=%async_computation.5 | async-start | bytes 2621440 | tf_op jit(solution)/shard_map/all_gather | solution.py:47
  234.1 3.7 copy-start.8
  340.1 106.7 %copy-start = (f32[512,1024]{0,1:T(8,128)S(1)}, f32[512,1024]{0,1:T(8,128)}, u32[]{:S(2)}) copy-start(f32[512,1024]{0,1:T(8,128)} %copy.238) | copy-start | bytes 6291460
  466.8 3.4 copy-start.10
  493.8 9.4 copy-start.14
  493.8 10.7 copy-start.16
  493.8 10.9 copy-start.15
  493.8 35.1 %all-to-all-start.1 = ((f32[4,512,128]{1,2,0:T(8,128)}), f32[4,512,128]{1,2,0:T(8,128)S(1)}, u32[]{:S(2)}, u32[]{:S(2)}) async-start(f32[4,512,128]{1,2,0:T(8,128)} %fusion.4), calls=%async_computation.1 | async-start | bytes 2097152 | tf_op jit(solution)/shard_map/all_to_all | solution.py:54
  509.3 2.5 copy-start.4
  528.9 18.9 %all-to-all-start = ((s32[64,1,2]{2,1,0:T(1,128)}), s32[64,1,2]{2,1,0:T(1,128)S(1)}, u32[]{:S(2)}, u32[]{:S(2)}) async-start(s32[64,1,2]{2,1,0:T(1,128)} %bitcast.67), calls=%async_computation | async-start | bytes 65536 | tf_op jit(solution)/shard_map/all_to_all | solution.py:78
  540.6 4.3 copy-start.1
  547.8 592.9 %all-to-all-start.2 = ((f32[64,2,128,128]{3,2,1,0:T(8,128)}), f32[64,2,128,128]{3,2,1,0:T(8,128)}, u32[]{:S(2)}, u32[]{:S(2)}) async-start(f32[64,2,128,128]{3,2,1,0:T(8,128)} %bitcast.457), calls=%async_computation.2 | async-start | bytes 16777216 | tf_op jit(solution)/shard_map/all_to_all | solution.py:71
  556.9 334.5 %all-reduce.6.cloned.1.call-start = ((), (), s32[]{:S(2)}) async-start(), calls=%async_computation.6 | async-start | bytes 8388608 | tf_op jit(solution)/shard_map/psum | solution.py:108
  955.1 2.9 copy-start.5
  962.1 0.7 copy-start.11
  1031.0 2.0 copy-start.2
  1031.9 1.1 copy-start.6
  1033.0 37.4 %copy-start.3 = (f32[128,512]{1,0:T(8,128)S(1)}, f32[128,512]{1,0:T(8,128)}, u32[]{:S(2)}) copy-start(f32[128,512]{1,0:T(8,128)} %copy-done.2) | copy-start | bytes 786436
  1033.1 37.4 %copy-start.7 = (f32[128,512]{1,0:T(8,128)S(1)}, f32[128,512]{1,0:T(8,128)}, u32[]{:S(2)}) copy-start(f32[128,512]{1,0:T(8,128)} %copy-done.6) | copy-start | bytes 786436
  1140.8 17.6 %copy-start.12 = (f32[512,256]{1,0:T(8,128)S(1)}, f32[512,256]{1,0:T(8,128)}, u32[]{:S(2)}) copy-start(f32[512,256]{1,0:T(8,128)} %param.64) | copy-start | bytes 1572868
  1159.3 111.9 %all-to-all-start.3 = ((f32[4,128,256]{2,1,0:T(8,128)}), f32[4,128,256]{2,1,0:T(8,128)S(1)}, u32[]{:S(2)}, u32[]{:S(2)}) async-start(f32[4,128,256]{2,1,0:T(8,128)} %bitcast.87), calls=%async_computation.3 | async-start | bytes 1048576 | tf_op jit(solution)/shard_map/all_to_all | solution.py:93
Sparse Core Ops, SparseCore 0:
  10.4 84.0 all-gather.2
  96.9 59.9 all-gather.4
  575.7 315.6 all-reduce.5
where the time goes:
time: 1300 us; the launch traced here: 1290 us
  other arithmetic  605 us (47%)
  waiting for transfers between devices  412 us (32%)
  local copies, waits for them, and re-layouts  128 us (10%)
  matrix products  85.6 us (7%)
  starting transfers between devices  34.5 us (3%)
  between operations  26.6 us (2%)
    psum x1, waiting for transfers between devices, shards(): whole_diag = lax.psum(placed - spread.reshape(W, W), ('front', 'blk'))  314 us
    another operation x18, other arithmetic, right_solve(): return jax.scipy.linalg.solve_triangular(factor, matrix.T, lower=True).T  290 us
    another operation x55, other arithmetic, blocked_cholesky(): diag_piece = jnp.linalg.cholesky(remaining[offset:finish, offset:finish])  278 us
    all_gather x1, waiting for transfers between devices, shards(): lax.all_gather(child_diag, 'blk', axis=0, tiled=True)  81.6 us
    another operation x63, matrix products, right_solve(): return jax.scipy.linalg.solve_triangular(factor, matrix.T, lower=True).T  61 us
    another operation x86, local copies, waits for them, and re-layouts, right_solve(): return jax.scipy.linalg.solve_triangular(factor, matrix.T, lower=True).T  48.4 us
    another operation x41, local copies, waits for them, and re-layouts  27.3 us
  transfers between devices with their start and end apart: 7, of which 3 were waited for; matrix products, arithmetic and copies ran while one was open for 58% of the time, Pallas kernels for 0%

commit v1 on v0

--- a/solution.py
+++ b/solution.py
@@ -1,3 +1,4 @@
+import functools
 import jax
 import jax.numpy as jnp
 from jax import lax
@@ -8,6 +9,15 @@
 TA = 4
 PB = 4
 HIGHEST = lax.Precision.HIGHEST
+
+
+def prepare_slot_now(local_array, peer_axis, d0):
+    back = jnp.stack([local_array] * lax.axis_size(peer_axis))
+    last = lax.all_to_all(back, axis_name=peer_axis, split_axis=0, concat_axis=0)
+    return jnp.concatenate(last, axis=d0)
+
+
+set_layers_all = functools.partial(prepare_slot_now, peer_axis="blk", d0=0)
 
 
 def right_solve(factor, matrix):
@@ -43,7 +53,7 @@
     block_width = W // TILE
     capacity = max(2, 8 * TA // front_count)
     diag_whole, top_whole = (
-        lax.all_gather(child_diag, "blk", axis=0, tiled=True),
+        set_layers_all(child_diag),
         lax.all_gather(child_top, "blk", axis=0, tiled=True),
     )
     factor = blocked_cholesky(diag_whole)

time: 1300 us -> 1370 us (1.054)
  waiting for transfers between devices: 412 us -> 455 us
    all_to_all x0 -> x1, waiting for transfers between devices: none -> 127 us  [prepare_slot_now(): lax.all_to_all(back, axis_name=peer_axis, split_axis=0, concat_axis=0)]
    all_gather x1 -> x0, waiting for transfers between devices: 81.6 us -> none  [shards(): lax.all_gather(child_diag, 'blk', axis=0, tiled=True)]
    another operation x41 -> x42, local copies, waits for them, and re-layouts: 27.3 us -> 29.6 us
  transfers between devices with their start and end apart: 7 -> 7, of which waited for: 3 -> 3; matrix products, arithmetic and copies ran while one was open for 58% -> 57% of each run, Pallas kernels for 0% -> 0%
where the time goes in v1:
time: 1370 us; the launch traced here: 1350 us
  other arithmetic  618 us (45%)
  waiting for transfers between devices  455 us (33%)
  local copies, waits for them, and re-layouts  132 us (10%)
  matrix products  85.3 us (6%)
  starting transfers between devices  35.8 us (3%)
  between operations  27 us (2%)
    psum x1, waiting for transfers between devices, shards(): whole_diag = lax.psum(placed - spread.reshape(W, W), ('front', 'blk'))  314 us
    another operation x18, other arithmetic, right_solve(): return jax.scipy.linalg.solve_triangular(factor, matrix.T, lower=True).T  303 us
    another operation x55, other arithmetic, blocked_cholesky(): diag_piece = jnp.linalg.cholesky(remaining[offset:finish, offset:finish])  278 us
    all_to_all x1, waiting for transfers between devices, prepare_slot_now(): lax.all_to_all(back, axis_name=peer_axis, split_axis=0, concat_axis=0)  127 us
    another operation x63, matrix products, right_solve(): return jax.scipy.linalg.solve_triangular(factor, matrix.T, lower=True).T  60.7 us
    another operation x86, local copies, waits for them, and re-layouts, right_solve(): return jax.scipy.linalg.solve_triangular(factor, matrix.T, lower=True).T  48.4 us
  transfers between devices with their start and end apart: 7, of which 3 were waited for; matrix products, arithmetic and copies ran while one was open for 57% of the time, Pallas kernels for 0%

profile of v1, /device:TPU:2, one launch (start us, length us, event | category | flops | bytes accessed | tf_op | source)
XLA Modules:
  0.0 1353.3 jit_solution(10305692180092666966)
XLA Ops:
  11.0 8.7 all-to-all-start
  22.6 126.7 %all-to-all-done = f32[4,256,1024]{1,2,0:T(8,128)} async-done(((f32[4,256,1024]{1,2,0:T(8,128)}), f32[4,256,1024]{1,2,0:T(8,128)}, u32[]{:S(2)}, u32[]{:S(2)}) %all-to-all-start) | async-done | bytes 4194336 | tf_op jit(solution)/shard_map/all_to_all | solution.py:16
  155.3 11.7 cholesky.382
  167.0 9.8 custom-call.38
  177.3 11.7 cholesky.399
  195.0 32.9 %custom-call.39 = f32[2,128,128]{1,2,0:T(8,128)S(1)} custom-call(f32[2,128,128]{2,1,0:T(8,128)S(1)} %get-tuple-element.311), custom_call_target="InvertDiagBlocksLowerTriangular" | custom-call | tf_op jit(solution)/shard_map/jit(_solve_triangular)/triangular_solve | solution.py:24
  239.2 11.7 cholesky.416
  250.9 10.4 custom-call.40
  262.7 11.7 cholesky.433
  282.0 20.1 %custom-call.41 = f32[2,128,128]{1,2,0:T(8,128)S(1)} custom-call(f32[2,128,128]{2,1,0:T(8,128)S(1)} %get-tuple-element.312), custom_call_target="InvertDiagBlocksLowerTriangular" | custom-call | tf_op jit(solution)/shard_map/jit(_solve_triangular)/triangular_solve | solution.py:24
  309.3 11.7 cholesky.450
  321.0 9.8 custom-call.42
  331.3 11.7 cholesky.467
  350.7 19.9 %custom-call.43 = f32[2,128,128]{1,2,0:T(8,128)S(1)} custom-call(f32[2,128,128]{2,1,0:T(8,128)S(1)} %get-tuple-element.313), custom_call_target="InvertDiagBlocksLowerTriangular" | custom-call | tf_op jit(solution)/shard_map/jit(_solve_triangular)/triangular_solve | solution.py:24
  372.2 11.7 cholesky.484
  384.0 9.8 custom-call.44
  394.3 11.7 cholesky.501
  410.2 4.8 fusion.1
  415.1 23.0 %while.41 = (s32[]{:T(128)}, f32[1024,1024]{1,0:T(8,128)}, s32[8,2]{0,1:T(2,128)S(1)}, f32[8,128,128]{2,1,0:T(8,128)S(1)}, s32[]{:T(128)}) while((s32[]{:T(128)}, f32[1024,1024]{1,0:T(8,128)}, s32[8,2]{0,1:T(2,128)S(1)}, f32[8,128,128]{2,1,0:T(8,128)S(1)}, s32[]{:T(128)}) %tuple.338), condition=%wide.while_cond.23, body=%wide.while_body.23.sunk | while | flops 2 | bytes 131181 | solution.py:24
  438.1 79.0 %custom-call.45 = f32[8,128,128]{1,2,0:T(8,128)S(1)} custom-call(f32[8,128,128]{2,1,0:T(8,128)S(1)} %get-tuple-element.314), custom_call_target="InvertDiagBlocksLowerTriangular" | custom-call | tf_op jit(solution)/shard_map/jit(_solve_triangular)/triangular_solve | solution.py:24
  557.3 6.7 fusion.4
  577.4 13.5 all-to-all-done.2
  590.8 8.8 all-to-all-start.1
  601.0 4.3 broadcast_in_dim.27
  608.2 9.0 all-to-all-start.3
  623.5 5.7 copy.215
  629.2 7.0 bitcast_subtract_fusion
  637.6 314.5 %all-reduce.6.cloned.1.call-done = f32[1024,1024]{0,1:T(8,128)} async-done(((f32[1024,1024]{0,1:T(8,128)}), f32[1024,1024]{0,1:T(8,128)}) %all-reduce.6.cloned.1.call-update) | async-done | bytes 4194320 | tf_op jit(solution)/shard_map/psum | solution.py:118
  954.2 11.7 cholesky.518
  966.0 9.8 custom-call.46
  976.4 11.7 cholesky.535
  995.9 19.7 %custom-call.47 = f32[2,128,128]{1,2,0:T(8,128)S(1)} custom-call(f32[2,128,128]{2,1,0:T(8,128)S(1)} %get-tuple-element.315), custom_call_target="InvertDiagBlocksLowerTriangular" | custom-call | tf_op jit(solution)/shard_map/jit(_solve_triangular)/triangular_solve | solution.py:24
  1023.4 11.7 cholesky.552
  1035.2 9.8 custom-call.48
  1047.3 12.1 cholesky.569
  1071.6 19.7 %custom-call.49 = f32[2,128,128]{1,2,0:T(8,128)S(1)} custom-call(f32[2,128,128]{2,1,0:T(8,128)S(1)} %get-tuple-element.316), custom_call_target="InvertDiagBlocksLowerTriangular" | custom-call | tf_op jit(solution)/shard_map/jit(_solve_triangular)/triangular_solve | solution.py:24
  1094.0 11.7 cholesky.586
  1105.8 9.8 custom-call.50
  1116.2 11.9 cholesky.603
  1136.8 19.7 %custom-call.51 = f32[2,128,128]{1,2,0:T(8,128)S(1)} custom-call(f32[2,128,128]{2,1,0:T(8,128)S(1)} %get-tuple-element.317), custom_call_target="InvertDiagBlocksLowerTriangular" | custom-call | tf_op jit(solution)/shard_map/jit(_solve_triangular)/triangular_solve | solution.py:24
  1158.3 11.7 cholesky.620
  1170.1 9.8 custom-call.52
  1180.5 11.7 cholesky.637
  1196.5 4.7 fusion
  1201.3 17.2 %scatter_fusion.2 = f32[8,128,128]{2,1,0:T(8,128)S(1)} fusion(f32[8,128,128]{2,1,0:T(8,128)S(1)} %broadcast.608.clone.1, s32[128]{0:T(128)S(1)} %fusion.185, f32[128,128,128]{2,1,0:T(8,128)} %bitcast.84), kind=kCustom, calls=%fused_computation.3 | custom fusion | flops 2097152 | bytes 25166336 | tf_op jit(solution)/shard_map/scatter-add | solution.py:95
  1219.8 5.6 all-to-all-start.4
  1225.4 25.1 %while.37 = (s32[]{:T(128)}, f32[1024,1024]{0,1:T(8,128)}, s32[8,2]{0,1:T(2,128)S(1)}, f32[8,128,128]{2,1,0:T(8,128)S(1)}, s32[]{:T(128)}) while((s32[]{:T(128)}, f32[1024,1024]{0,1:T(8,128)}, s32[8,2]{0,1:T(2,128)S(1)}, f32[8,128,128]{2,1,0:T(8,128)S(1)}, s32[]{:T(128)}) %tuple.357), condition=%wide.while_cond.24, body=%wide.while_body.24.sunk | while | flops 2 | bytes 393321 | solution.py:24
  1250.5 78.6 %custom-call.24 = f32[8,128,128]{1,2,0:T(8,128)S(1)} custom-call(f32[8,128,128]{2,1,0:T(8,128)S(1)} %get-tuple-element.286), custom_call_target="InvertDiagBlocksLowerTriangular" | custom-call | tf_op jit(solution)/shard_map/jit(_solve_triangular)/triangular_solve | solution.py:24
  (405 shorter events, 256.3 us)
Async XLA Ops:
  11.0 8.7 copy-start.14
  11.0 9.8 copy-start.10
  11.0 138.3 %all-to-all-start = ((f32[4,256,1024]{1,2,0:T(8,128)}), f32[4,256,1024]{1,2,0:T(8,128)}, u32[]{:S(2)}, u32[]{:S(2)}) async-start(f32[4,256,1024]{1,2,0:T(8,128)} %stack.2), calls=%async_computation | async-start | bytes 8388608 | tf_op jit(solution)/shard_map/all_to_all | solution.py:16
  19.8 517.5 %all-gather.2.cloned.1.call-start = ((), (), s32[]{:S(2)}) async-start(), calls=%async_computation.5 | async-start | bytes 2621440 | tf_op jit(solution)/shard_map/all_gather | solution.py:57
  152.1 1.9 copy-start
  304.5 3.7 copy-start.9
  410.2 106.9 %copy-start.1 = (f32[512,1024]{0,1:T(8,128)S(1)}, f32[512,1024]{0,1:T(8,128)}, u32[]{:S(2)}) copy-start(f32[512,1024]{0,1:T(8,128)} %copy.240) | copy-start | bytes 6291460
  537.2 3.4 copy-start.11
  564.0 3.7 copy-start.15
  564.0 5.0 copy-start.17
  564.0 5.2 copy-start.16
  564.0 26.8 %all-to-all-start.2 = ((f32[4,512,128]{1,2,0:T(8,128)}), f32[4,512,128]{1,2,0:T(8,128)S(1)}, u32[]{:S(2)}, u32[]{:S(2)}) async-start(f32[4,512,128]{1,2,0:T(8,128)} %fusion.4), calls=%async_computation.2 | async-start | bytes 2097152 | tf_op jit(solution)/shard_map/all_to_all | solution.py:64
  573.8 2.5 copy-start.5
  590.8 17.4 %all-to-all-start.1 = ((s32[64,1,2]{2,1,0:T(1,128)}), s32[64,1,2]{2,1,0:T(1,128)S(1)}, u32[]{:S(2)}, u32[]{:S(2)}) async-start(s32[64,1,2]{2,1,0:T(1,128)} %bitcast.67), calls=%async_computation.1 | async-start | bytes 65536 | tf_op jit(solution)/shard_map/all_to_all | solution.py:88
  601.0 4.3 copy-start.2
  608.2 593.0 %all-to-all-start.3 = ((f32[64,2,128,128]{3,2,1,0:T(8,128)}), f32[64,2,128,128]{3,2,1,0:T(8,128)}, u32[]{:S(2)}, u32[]{:S(2)}) async-start(f32[64,2,128,128]{3,2,1,0:T(8,128)} %bitcast.459), calls=%async_computation.3 | async-start | bytes 16777216 | tf_op jit(solution)/shard_map/all_to_all | solution.py:81
  617.3 334.8 %all-reduce.6.cloned.1.call-start = ((), (), s32[]{:S(2)}) async-start(), calls=%async_computation.6 | async-start | bytes 8388608 | tf_op jit(solution)/shard_map/psum | solution.py:118
  1015.6 2.9 copy-start.6
  1022.6 0.7 copy-start.12
  1091.8 2.0 copy-start.3
  1092.6 1.1 copy-start.7
  1093.8 37.1 %copy-start.4 = (f32[128,512]{1,0:T(8,128)S(1)}, f32[128,512]{1,0:T(8,128)}, u32[]{:S(2)}) copy-start(f32[128,512]{1,0:T(8,128)} %copy-done.3) | copy-start | bytes 786436
  1093.8 37.1 %copy-start.8 = (f32[128,512]{1,0:T(8,128)S(1)}, f32[128,512]{1,0:T(8,128)}, u32[]{:S(2)}) copy-start(f32[128,512]{1,0:T(8,128)} %copy-done.7) | copy-start | bytes 786436
  1201.3 17.7 %copy-start.13 = (f32[512,256]{1,0:T(8,128)S(1)}, f32[512,256]{1,0:T(8,128)}, u32[]{:S(2)}) copy-start(f32[512,256]{1,0:T(8,128)} %param.64) | copy-start | bytes 1572868
  1219.8 111.9 %all-to-all-start.4 = ((f32[4,128,256]{2,1,0:T(8,128)}), f32[4,128,256]{2,1,0:T(8,128)S(1)}, u32[]{:S(2)}, u32[]{:S(2)}) async-start(f32[4,128,256]{2,1,0:T(8,128)} %bitcast.87), calls=%async_computation.4 | async-start | bytes 1048576 | tf_op jit(solution)/shard_map/all_to_all | solution.py:103
Sparse Core Ops, SparseCore 0:
  23.0 118.3 all-gather.1
  636.3 315.6 all-reduce.5
